TPU v7x, 32 devices: a whole 2x2x4 slice. The times are simulated.
32 devices in a mesh: ens: 2 (over y), lon: 4 (over z), lat: 4 (over x, core).
Axes of the slice: x: 2, y: 2, z: 4, core: 2. Of those that a mesh axis runs over, the one named last changes fastest.
Arguments:
- field: float32 [8, 1440, 640], P(('ens', 'lat'), 'lon'), parts along dimension 0, may hold values from -6 to 6
- piece_lengths: int32 [4], replicated, may hold values from 1 to 360, 720 in all
- offsets: int32 [4], replicated, may hold values from 0 to 2, as said below
- basis: float32 [9, 4, 2, 17], replicated, may hold values from -1 to 1
- depth_weight: float32 [9, 640], replicated, may hold values from -2 to 2
- gain: float32 [640], replicated, may hold values from 0.5 to 1.5
- w_in: bfloat16 [640, 1280], replicated, may hold values from -0.25 to 0.25
- b_in: float32 [1280], replicated, may hold values from -3 to 3
- w_out: bfloat16 [1280, 640], replicated, may hold values from -0.15625 to 0.15625
- b_out: float32 [640], replicated, may hold values from -3 to 3
Outputs:
- result: float32 [8, 1440, 640], P(('ens', 'lat'), 'lon'), parts along dimension 0
There are 2 independent parts, one for each index of `ens`. A program takes and returns all parts, laid end to end along the dimension named above; an argument that names none is the same for every part. Nothing has to cross between parts.
Inputs may be any that keep to these rules, and one draw needn't show every extreme that they name: Index b of lon holds longitudes starts[b] to starts[b] + piece_lengths[b] - 1 in its first piece_lengths[b] slots; the lengths sum to 720. Output row i reads latitude rows offsets[i] to offsets[i] + 1, and i - 1 <= offsets[i] <= i.
All inputs are finite; a program needn't handle non-finite values.
Results may differ from a plain program's by a relative error of at most 0.0018.
Values sent between devices are 32-bit elements; how exact they have to be, the bound alone decides.
A program may use at most 64 MiB of HBM per device.

v0:
```python
import functools
import jax
import jax.numpy as jnp
from jax import lax
from jax.experimental import pallas as pl
from jax.experimental.pallas import tpu as pltpu
from jax.sharding import PartitionSpec as P

LANES = 128
HALO = 8
MESH = pl.DeviceIdType.MESH
SQRT_HALF = 0.7071067811865476


def round_up(value, step):
    return -(-value // step) * step


def block_rows(total, most):
    return max(rows for rows in range(8, most + 1, 8) if total % rows == 0)


def kernel(
    groups, lat_count, n, hid_block,
    lengths_hbm, offsets_hbm, field, basis_hbm, depth_hbm, gain_hbm, w_in_hbm, b_in_hbm, w_out_hbm, b_out_hbm,
    out_hbm,
    lengths, offsets, basis, depth_weight, gain, b_in, b_out,
    raw, edge, peers, halo, nb, nb_halo, ext, ext_nb, tail, terms, coef, acc, st, out_buf, w_in, w_out,
    load_sem, small_sem, weight_sem, edge_send, edge_recv, halo_send, halo_recv, row_send, row_recv, out_sem,
):
    cap = raw.shape[1]
    tiles = raw.shape[0]
    channels = tiles * LANES
    taps = basis.shape[3]
    count_k = basis.shape[0]
    blocks = cap // n
    hidden = w_in.shape[1]
    g = lax.axis_index("lon")
    t = lax.axis_index("lat")
    above, below = t < lat_count - 1, t > 0

    loads = [
        pltpu.make_async_copy(field.at[0, :, pl.ds(k * LANES, LANES)], raw.at[k], load_sem.at[k])
        for k in range(tiles)
    ]
    weights = [
        pltpu.make_async_copy(w_in_hbm, w_in, weight_sem.at[0]),
        pltpu.make_async_copy(w_out_hbm, w_out, weight_sem.at[1]),
    ]
    pairs = [
        (lengths_hbm, lengths), (offsets_hbm, offsets), (basis_hbm, basis), (depth_hbm, depth_weight),
        (gain_hbm, gain.at[0]), (b_in_hbm, b_in.at[0]), (b_out_hbm, b_out.at[0]),
    ]
    smalls = [pltpu.make_async_copy(source, target, small_sem.at[i]) for i, (source, target) in enumerate(pairs)]
    for copy in loads + smalls + weights:
        copy.start()

    barrier = pltpu.get_barrier_semaphore()

    @pl.when(above)
    def _():
        pl.semaphore_signal(barrier, inc=1, device_id={"lat": t + 1}, device_id_type=MESH)

    @pl.when(below)
    def _():
        pl.semaphore_signal(barrier, inc=1, device_id={"lat": t - 1}, device_id_type=MESH)

    for d in range(1, groups):
        pl.semaphore_signal(barrier, inc=1, device_id={"lon": lax.rem(g + d, groups)}, device_id_type=MESH)

    tail[...] = jnp.zeros_like(tail)
    for target in (ext, ext_nb):
        target[:, 0:HALO, :] = jnp.zeros((tiles, HALO, LANES), jnp.float32)
        target[:, cap + HALO:cap + 2 * HALO, :] = jnp.zeros((tiles, HALO, LANES), jnp.float32)

    smalls[0].wait()
    length = lengths[g]
    for copy in loads:
        copy.wait()
    edge[:, 0:HALO, :] = raw[:, 0:HALO, :]
    for k in range(tiles):
        edge[k, HALO:2 * HALO, :] = raw[k, pl.ds(jnp.maximum(length - HALO, 0), HALO), :]

    pl.semaphore_wait(barrier, groups - 1 + above.astype(jnp.int32) + below.astype(jnp.int32))

    def edge_copy(d):
        return pltpu.make_async_remote_copy(
            src_ref=edge, dst_ref=peers.at[d], send_sem=edge_send.at[d], recv_sem=edge_recv.at[d],
            device_id={"lon": lax.rem(g + d, groups)}, device_id_type=MESH,
        )

    def span(c):
        first = 0 if c == 0 else c * n + HALO
        last = cap if c == blocks - 1 else (c + 1) * n + HALO
        return first, last

    def row_copy(side, c):
        first, last = span(c)
        rows = pl.ds(first, last - first)
        return pltpu.make_async_remote_copy(
            src_ref=raw.at[:, rows, :], dst_ref=nb.at[side, :, rows, :],
            send_sem=row_send.at[side, c], recv_sem=row_recv.at[side, c],
            device_id={"lat": t + 1 - 2 * side}, device_id_type=MESH,
        )

    def halo_copy(side):
        return pltpu.make_async_remote_copy(
            src_ref=halo, dst_ref=nb_halo.at[side], send_sem=halo_send.at[side], recv_sem=halo_recv.at[side],
            device_id={"lat": t + 1 - 2 * side}, device_id_type=MESH,
        )

    odd = lax.rem(t, 2) == 1

    def sends(act):
        for side, exists in ((0, above & odd), (1, below & ~odd), (0, above & ~odd), (1, below & odd)):
            pl.when(exists)(functools.partial(act, side))

    def receives(act):
        for side, exists in ((0, below), (1, above)):
            pl.when(exists)(functools.partial(act, side))

    for d in range(1, groups):
        edge_copy(d).start()
    sends(lambda side: row_copy(side, 0).start())

    for copy in smalls[1:]:
        copy.wait()
    use_above = offsets[t] == t
    terms[...] = jnp.zeros_like(terms)
    for s in range(2):
        for k in range(count_k):
            terms[s, k:k + 1, 0:taps] = basis[k, t, s:s + 1, :]
    weight = jnp.concatenate([depth_weight[...], jnp.zeros((terms.shape[1] - count_k, channels), jnp.float32)], 0)
    both = [
        lax.dot_general(
            terms[s], weight, (((0,), (0,)), ((), ())),
            precision=lax.Precision.HIGHEST, preferred_element_type=jnp.float32,
        )
        for s in range(2)
    ]
    own_coef = jnp.where(use_above, both[0], both[1])
    nb_coef = jnp.where(use_above, both[1], both[0])
    for k in range(tiles):
        coef[0, k] = own_coef[:, k * LANES:(k + 1) * LANES]
        coef[1, k] = nb_coef[:, k * LANES:(k + 1) * LANES]

    def conv(source, which, k, start):
        total = None
        for shift in range(HALO):
            reach = n + HALO * ((taps - 1 - shift) // HALO)
            moved = source[k, start + shift:start + shift + reach, :]
            for tap in range(shift, taps, HALO):
                term = moved[tap - shift:tap - shift + n] * coef[which, k, tap:tap + 1, :]
                total = term if total is None else total + term
        return total

    def extend(target, values, c):
        first, last = span(c)

        def tile(k, carry):
            inside = first + lax.broadcasted_iota(jnp.int32, (last - first, LANES), 0) < length
            target[k, HALO + first:HALO + last, :] = jnp.where(inside, values(k, first, last), 0.0)
            return carry

        lax.fori_loop(0, tiles, tile, 0)

    def own_block(c):
        def own_tile(k, carry):
            acc[k, c * n:(c + 1) * n, :] = raw[k, c * n:(c + 1) * n, :] + conv(ext, 0, k, c * n)
            return carry

        lax.fori_loop(0, tiles, own_tile, 0)

    for c in range(blocks):
        extend(ext, lambda k, a, b: raw[k, a:b, :], c)
    own_block(0)

    for d in range(1, groups):
        edge_copy(d).wait_recv()
    steps = min(HALO, groups - 1)
    right = [(groups - 1 - q, lengths[lax.rem(g + 1 + q, groups)]) for q in range(steps)]
    left = [(1 + q, lengths[lax.rem(g + groups - 1 - q, groups)]) for q in range(steps)]
    for j in range(HALO):
        source, slot, passed = right[0][0], jnp.int32(j), jnp.int32(0)
        for q in range(1, steps):
            passed = passed + right[q - 1][1]
            source = jnp.where(passed <= j, right[q][0], source)
            slot = jnp.where(passed <= j, j - passed, slot)
        halo[:, HALO + j:HALO + j + 1, :] = peers[source, :, pl.ds(slot, 1), :]
        back = HALO - j
        source, row, passed = left[0][0], HALO + jnp.minimum(left[0][1], HALO) - back, jnp.int32(0)
        for q in range(1, steps):
            passed = passed + left[q - 1][1]
            reach = passed < back
            source = jnp.where(reach, left[q][0], source)
            row = jnp.where(reach, HALO + jnp.minimum(left[q][1], HALO) - (back - passed), row)
        halo[:, j:j + 1, :] = peers[source, :, pl.ds(jnp.maximum(row, 0), 1), :]

    sends(lambda side: halo_copy(side).start())
    for c in range(1, blocks):
        sends(lambda side: row_copy(side, c).start())
    for c in range(1, blocks):
        own_block(c)

    receives(lambda side: halo_copy(side).wait_recv())
    around = jnp.zeros((2 * HALO, LANES), jnp.float32)
    for k in range(tiles):
        near = jnp.where(use_above, nb_halo[1, k], nb_halo[0, k])
        from_left, from_right = None, None
        for which, values in ((0, halo[k]), (1, near)):
            lefts = jnp.concatenate([values[0:HALO], around], axis=0)
            rights = jnp.concatenate([around, values[HALO:2 * HALO]], axis=0)
            for tap in range(taps):
                factor = coef[which, k, tap:tap + 1, :]
                if tap < HALO:
                    term = lefts[tap:tap + HALO] * factor
                    from_left = term if from_left is None else from_left + term
                if tap > HALO:
                    term = rights[tap:tap + HALO] * factor
                    from_right = term if from_right is None else from_right + term
        acc[k, 0:HALO, :] += from_left
        tail[k, cap - HALO:cap, :] = from_right
    for copy in weights:
        copy.wait()

    writes = []
    for c in range(blocks):
        receives(lambda side: row_copy(side, c).wait_recv())
        extend(ext_nb, lambda k, a, b: jnp.where(use_above, nb[1, k, a:b, :], nb[0, k, a:b, :]), c)

        def nb_tile(k, squares):
            state = acc[k, c * n:(c + 1) * n, :] + conv(ext_nb, 1, k, c * n) + tail[k, pl.ds(cap + c * n - length, n), :]
            st[k] = state
            return squares + state * state

        squares = lax.fori_loop(0, tiles, nb_tile, jnp.zeros((n, LANES), jnp.float32))
        scale = lax.rsqrt(jnp.sum(squares, axis=1, keepdims=True) * (1.0 / channels) + 1e-05)
        state = jnp.concatenate([st[k] for k in range(tiles)], axis=1)
        normed = (state * scale * gain[...]).astype(jnp.bfloat16)
        total = state + b_out[...]
        for h in range(0, hidden, hid_block):
            pre = jnp.dot(normed, w_in[:, h:h + hid_block], preferred_element_type=jnp.float32) + b_in[:, h:h + hid_block]
            active = (0.5 * pre * (1.0 + lax.erf(pre * SQRT_HALF))).astype(jnp.bfloat16)
            total = total + jnp.dot(active, w_out[h:h + hid_block, :], preferred_element_type=jnp.float32)
        inside = c * n + lax.broadcasted_iota(jnp.int32, total.shape, 0) < length
        out_buf[c * n:(c + 1) * n, :] = jnp.where(inside, total, 0.0)
        write = pltpu.make_async_copy(
            out_buf.at[pl.ds(c * n, n), :], out_hbm.at[0, pl.ds(c * n, n), :], out_sem.at[c]
        )
        write.start()
        writes.append(write)

    for d in range(1, groups):
        edge_copy(d).wait_send()
    sends(lambda side: halo_copy(side).wait_send())
    for c in range(blocks):
        sends(lambda side: row_copy(side, c).wait_send())
    for write in writes:
        write.wait()


def on_device(groups, lat_count, field, piece_lengths, offsets, basis, depth_weight, gain, w_in, b_in, w_out, b_out):
    rows_dev, slot_cap, channels = field.shape
    assert rows_dev == 1 and basis.shape[2] == 2 and basis.shape[3] == 2 * HALO + 1
    cap = round_up(slot_cap, 8)
    if cap != slot_cap:
        field = jnp.pad(field, ((0, 0), (0, cap - slot_cap), (0, 0)))
    tiles = channels // LANES
    hidden = w_in.shape[1]
    n = block_rows(cap, 120)
    blocks = cap // n
    hid_block = 256 if hidden % 256 == 0 else LANES
    taps = basis.shape[3]
    k_rows = round_up(basis.shape[0], 8)
    hbm = pl.BlockSpec(memory_space=pltpu.HBM)
    f32 = jnp.float32
    out = pl.pallas_call(
        functools.partial(kernel, groups, lat_count, n, hid_block),
        out_shape=jax.ShapeDtypeStruct((1, cap, channels), f32),
        in_specs=[hbm] * 10,
        out_specs=pl.BlockSpec(memory_space=pl.ANY),
        scratch_shapes=[
            pltpu.SMEM(piece_lengths.shape, jnp.int32),
            pltpu.SMEM(offsets.shape, jnp.int32),
            pltpu.VMEM(basis.shape, f32),
            pltpu.VMEM(depth_weight.shape, f32),
            pltpu.VMEM((1, channels), f32),
            pltpu.VMEM((1, hidden), f32),
            pltpu.VMEM((1, channels), f32),
            pltpu.VMEM((tiles, cap, LANES), f32),
            pltpu.VMEM((tiles, 2 * HALO, LANES), f32),
            pltpu.VMEM((groups, tiles, 2 * HALO, LANES), f32),
            pltpu.VMEM((tiles, 2 * HALO, LANES), f32),
            pltpu.VMEM((2, tiles, cap, LANES), f32),
            pltpu.VMEM((2, tiles, 2 * HALO, LANES), f32),
            pltpu.VMEM((tiles, cap + 2 * HALO, LANES), f32),
            pltpu.VMEM((tiles, cap + 2 * HALO, LANES), f32),
            pltpu.VMEM((tiles, 2 * cap + 2 * HALO, LANES), f32),
            pltpu.VMEM((2, k_rows, round_up(taps, 8)), f32),
            pltpu.VMEM((2, tiles, round_up(taps, 8), LANES), f32),
            pltpu.VMEM((tiles, cap, LANES), f32),
            pltpu.VMEM((tiles, n, LANES), f32),
            pltpu.VMEM((cap, channels), f32),
            pltpu.VMEM(w_in.shape, w_in.dtype),
            pltpu.VMEM(w_out.shape, w_out.dtype),
            pltpu.SemaphoreType.DMA((tiles,)),
            pltpu.SemaphoreType.DMA((7,)),
            pltpu.SemaphoreType.DMA((2,)),
            pltpu.SemaphoreType.DMA((groups,)),
            pltpu.SemaphoreType.DMA((groups,)),
            pltpu.SemaphoreType.DMA((2,)),
            pltpu.SemaphoreType.DMA((2,)),
            pltpu.SemaphoreType.DMA((2, blocks)),
            pltpu.SemaphoreType.DMA((2, blocks)),
            pltpu.SemaphoreType.DMA((blocks,)),
        ],
        compiler_params=pltpu.CompilerParams(
            collective_id=0, has_side_effects=True, vmem_limit_bytes=63 * 1024 * 1024
        ),
        cost_estimate=pl.CostEstimate(flops=4 * cap * channels * hidden, bytes_accessed=6 * 1024 * 1024, transcendentals=0),
    )(
        piece_lengths, offsets, field, basis, depth_weight, gain, w_in, b_in, w_out, b_out,
    )
    return out[:, :slot_cap, :]


def solution(mesh):
    placed = (P(("ens", "lat"), "lon", None), P(), P(), P(), P(), P(), P(), P(), P(), P())
    return jax.shard_map(
        functools.partial(on_device, mesh.shape["lon"], mesh.shape["lat"]),
        mesh=mesh,
        in_specs=placed,
        out_specs=P(("ens", "lat"), "lon", None),
        check_vma=False,
    )
```

profile of v0, /device:TPU:1, one launch (start us, length us, event | category | flops | bytes accessed | tf_op | source)
XLA Modules:
  0.0 23.3 jit_solution(5137614657426753986)
XLA Ops:
  0.0 21.1 %shard_map.100 = f32[1,360,640]{2,1,0:T(8,128)} custom-call(s32[4]{0:T(128)} %lengths_hbm.1, s32[4]{0:T(128)} %offsets_hbm.1, f32[1,360,640]{2,1,0:T(8,128)} %field.1, f32[9,4,2,17]{3,2,1,0:T(2,128)} %basis_hbm.1, f32[9,640]{1,0:T(8,128)} %depth_hbm.1, f32[640]{0:T(1024)} %gain_hbm.1, bf16[640,1280]{1,0:T(8,128)(2,1)} %w_in_hbm.1, f32[1280]{0:T(1024)} %b_in_hbm.1, ...), custom_call_target="tpu_custom_call" | custom-call | flops 1179648000 | bytes 6291456 | tf_op jit(solution)/shard_map/pallas_call | solution.py:277
  21.1 2.2 %copy.12 = f32[1,360,640]{2,1,0:T(8,128)} copy(f32[1,360,640]{2,1,0:T(8,128)} %shard_map.100) | data formatting | bytes 1843200
where the time goes:
time: 23.4 us; the launch traced here: 23.3 us
  Pallas kernels  21.1 us (90%)
  local copies, waits for them, and re-layouts  2.16 us (9%)
    pallas_call x1, Pallas kernels, on_device(): pl.pallas_call(functools.partial(kernel, groups, lat_count, n, hid_block)...  21.1 us
    unnamed x1, local copies, waits for them, and re-layouts  2.16 us

commit v1 on v0

--- a/solution.py
+++ b/solution.py
@@ -26,7 +26,7 @@
     out_hbm,
     lengths, offsets, basis, depth_weight, gain, b_in, b_out,
     raw, edge, peers, halo, nb, nb_halo, ext, ext_nb, tail, terms, coef, acc, st, out_buf, w_in, w_out,
-    load_sem, small_sem, weight_sem, edge_send, edge_recv, halo_send, halo_recv, row_send, row_recv, out_sem,
+    load_sem, small_sem, weight_sem, edge_send, edge_recv, halo_send, halo_recv, row_send, row_recv, pass_send, out_sem,
 ):
     cap = raw.shape[1]
     tiles = raw.shape[0]
@@ -65,6 +65,14 @@
     def _():
         pl.semaphore_signal(barrier, inc=1, device_id={"lat": t - 1}, device_id_type=MESH)
 
+    @pl.when(t + 2 < lat_count)
+    def _():
+        pl.semaphore_signal(barrier, inc=1, device_id={"lat": t + 2}, device_id_type=MESH)
+
+    @pl.when(t >= 2)
+    def _():
+        pl.semaphore_signal(barrier, inc=1, device_id={"lat": t - 2}, device_id_type=MESH)
+
     for d in range(1, groups):
         pl.semaphore_signal(barrier, inc=1, device_id={"lon": lax.rem(g + d, groups)}, device_id_type=MESH)
 
@@ -81,7 +89,8 @@
     for k in range(tiles):
         edge[k, HALO:2 * HALO, :] = raw[k, pl.ds(jnp.maximum(length - HALO, 0), HALO), :]
 
-    pl.semaphore_wait(barrier, groups - 1 + above.astype(jnp.int32) + below.astype(jnp.int32))
+    greeted = [above, below, t + 2 < lat_count, t >= 2]
+    pl.semaphore_wait(barrier, groups - 1 + sum(near.astype(jnp.int32) for near in greeted))
 
     def edge_copy(d):
         return pltpu.make_async_remote_copy(
@@ -94,13 +103,23 @@
         last = cap if c == blocks - 1 else (c + 1) * n + HALO
         return first, last
 
-    def row_copy(side, c):
+    def half(c, h):
         first, last = span(c)
-        rows = pl.ds(first, last - first)
+        middle = first + round_up((last - first) // 2, 8)
+        return pl.ds(first, middle - first) if h == 0 else pl.ds(middle, last - middle)
+
+    def row_copy(side, c, h):
         return pltpu.make_async_remote_copy(
-            src_ref=raw.at[:, rows, :], dst_ref=nb.at[side, :, rows, :],
-            send_sem=row_send.at[side, c], recv_sem=row_recv.at[side, c],
+            src_ref=raw.at[:, half(c, h), :], dst_ref=nb.at[side, :, half(c, h), :],
+            send_sem=row_send.at[side, c, h], recv_sem=row_recv.at[side, c, h],
             device_id={"lat": t + 1 - 2 * side}, device_id_type=MESH,
+        )
+
+    def pass_copy(side, c):
+        return pltpu.make_async_remote_copy(
+            src_ref=nb.at[1 - side, :, half(c, 1), :], dst_ref=nb.at[side, :, half(c, 1), :],
+            send_sem=pass_send.at[c], recv_sem=row_recv.at[side, c, 1],
+            device_id={"lat": t + 2 - 4 * side}, device_id_type=MESH,
         )
 
     def halo_copy(side):
@@ -111,17 +130,39 @@
 
     odd = lax.rem(t, 2) == 1
 
-    def sends(act):
-        for side, exists in ((0, above & odd), (1, below & ~odd), (0, above & ~odd), (1, below & odd)):
-            pl.when(exists)(functools.partial(act, side))
-
-    def receives(act):
-        for side, exists in ((0, below), (1, above)):
-            pl.when(exists)(functools.partial(act, side))
+    def crossing(act):
+        pl.when(above & odd)(functools.partial(act, 0))
+        pl.when(below & ~odd)(functools.partial(act, 1))
+
+    def crossed(act):
+        pl.when(above & odd)(functools.partial(act, 1))
+        pl.when(below & ~odd)(functools.partial(act, 0))
+
+    def to_mate(act):
+        pl.when(~odd)(functools.partial(act, 0))
+        pl.when(odd)(functools.partial(act, 1))
+
+    def from_mate(act):
+        pl.when(~odd)(functools.partial(act, 1))
+        pl.when(odd)(functools.partial(act, 0))
+
+    def passing(act):
+        pl.when(~odd & (t + 2 < lat_count))(functools.partial(act, 0))
+        pl.when(odd & (t >= 2))(functools.partial(act, 1))
+
+    def send_block(c):
+        crossing(lambda side: row_copy(side, c, 0).start())
+        to_mate(lambda side: row_copy(side, c, 1).start())
+        to_mate(lambda side: row_copy(side, c, 0).start())
+
+    def pass_block(c):
+        from_mate(lambda side: row_copy(side, c, 1).wait_recv())
+        passing(lambda side: pass_copy(side, c).start())
 
     for d in range(1, groups):
         edge_copy(d).start()
-    sends(lambda side: row_copy(side, 0).start())
+    for c in range(max(1, blocks - 1)):
+        send_block(c)
 
     for copy in smalls[1:]:
         copy.wait()
@@ -173,6 +214,7 @@
 
     for c in range(blocks):
         extend(ext, lambda k, a, b: raw[k, a:b, :], c)
+    pass_block(0)
     own_block(0)
 
     for d in range(1, groups):
@@ -196,13 +238,16 @@
             row = jnp.where(reach, HALO + jnp.minimum(left[q][1], HALO) - (back - passed), row)
         halo[:, j:j + 1, :] = peers[source, :, pl.ds(jnp.maximum(row, 0), 1), :]
 
-    sends(lambda side: halo_copy(side).start())
+    crossing(lambda side: halo_copy(side).start())
+    to_mate(lambda side: halo_copy(side).start())
+    for c in range(max(1, blocks - 1), blocks):
+        send_block(c)
     for c in range(1, blocks):
-        sends(lambda side: row_copy(side, c).start())
-    for c in range(1, blocks):
+        pass_block(c)
         own_block(c)
 
-    receives(lambda side: halo_copy(side).wait_recv())
+    crossed(lambda side: halo_copy(side).wait_recv())
+    from_mate(lambda side: halo_copy(side).wait_recv())
     around = jnp.zeros((2 * HALO, LANES), jnp.float32)
     for k in range(tiles):
         near = jnp.where(use_above, nb_halo[1, k], nb_halo[0, k])
@@ -225,7 +270,9 @@
 
     writes = []
     for c in range(blocks):
-        receives(lambda side: row_copy(side, c).wait_recv())
+        from_mate(lambda side: row_copy(side, c, 0).wait_recv())
+        crossed(lambda side: row_copy(side, c, 0).wait_recv())
+        crossed(lambda side: row_copy(side, c, 1).wait_recv())
         extend(ext_nb, lambda k, a, b: jnp.where(use_above, nb[1, k, a:b, :], nb[0, k, a:b, :]), c)
 
         def nb_tile(k, squares):
@@ -243,7 +290,7 @@
             active = (0.5 * pre * (1.0 + lax.erf(pre * SQRT_HALF))).astype(jnp.bfloat16)
             total = total + jnp.dot(active, w_out[h:h + hid_block, :], preferred_element_type=jnp.float32)
         inside = c * n + lax.broadcasted_iota(jnp.int32, total.shape, 0) < length
-        out_buf[c * n:(c + 1) * n, :] = jnp.where(inside, total, 0.0)
+        out_buf[c * n:(c + 1) * n, :] = jnp.where(inside, -total, -0.0)
         write = pltpu.make_async_copy(
             out_buf.at[pl.ds(c * n, n), :], out_hbm.at[0, pl.ds(c * n, n), :], out_sem.at[c]
         )
@@ -252,16 +299,20 @@
 
     for d in range(1, groups):
         edge_copy(d).wait_send()
-    sends(lambda side: halo_copy(side).wait_send())
+    crossing(lambda side: halo_copy(side).wait_send())
+    to_mate(lambda side: halo_copy(side).wait_send())
     for c in range(blocks):
-        sends(lambda side: row_copy(side, c).wait_send())
+        crossing(lambda side: row_copy(side, c, 0).wait_send())
+        to_mate(lambda side: row_copy(side, c, 0).wait_send())
+        to_mate(lambda side: row_copy(side, c, 1).wait_send())
+        passing(lambda side: pass_copy(side, c).wait_send())
     for write in writes:
         write.wait()
 
 
 def on_device(groups, lat_count, field, piece_lengths, offsets, basis, depth_weight, gain, w_in, b_in, w_out, b_out):
     rows_dev, slot_cap, channels = field.shape
-    assert rows_dev == 1 and basis.shape[2] == 2 and basis.shape[3] == 2 * HALO + 1
+    assert rows_dev == 1 and lat_count % 2 == 0 and basis.shape[2] == 2 and basis.shape[3] == 2 * HALO + 1
     cap = round_up(slot_cap, 8)
     if cap != slot_cap:
         field = jnp.pad(field, ((0, 0), (0, cap - slot_cap), (0, 0)))
@@ -310,8 +361,9 @@
             pltpu.SemaphoreType.DMA((groups,)),
             pltpu.SemaphoreType.DMA((2,)),
             pltpu.SemaphoreType.DMA((2,)),
-            pltpu.SemaphoreType.DMA((2, blocks)),
-            pltpu.SemaphoreType.DMA((2, blocks)),
+            pltpu.SemaphoreType.DMA((2, blocks, 2)),
+            pltpu.SemaphoreType.DMA((2, blocks, 2)),
+            pltpu.SemaphoreType.DMA((blocks,)),
             pltpu.SemaphoreType.DMA((blocks,)),
         ],
         compiler_params=pltpu.CompilerParams(
@@ -321,7 +373,7 @@
     )(
         piece_lengths, offsets, field, basis, depth_weight, gain, w_in, b_in, w_out, b_out,
     )
-    return out[:, :slot_cap, :]
+    return -out[:, :slot_cap, :]
 
 
 def solution(mesh):

time: 23.4 us -> 22.9 us (0.979)
  other arithmetic: 0 us -> 2.17 us
  local copies, waits for them, and re-layouts: 2.16 us -> 0 us
  Pallas kernels: 21.1 us -> 20.5 us
    neg x0 -> x1, other arithmetic: none -> 2.17 us  [on_device(): return -out[:, :slot_cap, :]]
    unnamed x1 -> x0, local copies, waits for them, and re-layouts: 2.16 us -> none
    pallas_call x1, Pallas kernels: 21.1 us -> 20.5 us  [on_device(): pl.pallas_call(functools.partial(kernel, groups, lat_count, n, hid_block)...]
where the time goes in v1:
time: 22.9 us; the launch traced here: 22.7 us
  Pallas kernels  20.5 us (90%)
  other arithmetic  2.17 us (9%)
    pallas_call x1, Pallas kernels, on_device(): pl.pallas_call(functools.partial(kernel, groups, lat_count, n, hid_block)...  20.5 us
    neg x1, other arithmetic, on_device(): return -out[:, :slot_cap, :]  2.17 us

profile of v1, /device:TPU:1, one launch (start us, length us, event | category | flops | bytes accessed | tf_op | source)
XLA Modules:
  0.0 22.7 jit_solution(5130677127868330186)
XLA Ops:
  0.0 20.5 %shard_map.100 = f32[1,360,640]{2,1,0:T(8,128)} custom-call(s32[4]{0:T(128)} %lengths_hbm.1, s32[4]{0:T(128)} %offsets_hbm.1, f32[1,360,640]{2,1,0:T(8,128)} %field.1, f32[9,4,2,17]{3,2,1,0:T(2,128)} %basis_hbm.1, f32[9,640]{1,0:T(8,128)} %depth_hbm.1, f32[640]{0:T(1024)} %gain_hbm.1, bf16[640,1280]{1,0:T(8,128)(2,1)} %w_in_hbm.1, f32[1280]{0:T(1024)} %b_in_hbm.1, ...), custom_call_target="tpu_custom_call" | custom-call | flops 1179648000 | bytes 6291456 | tf_op jit(solution)/shard_map/pallas_call | solution.py:328
  20.6 2.2 %neg.3 = f32[1,360,640]{2,1,0:T(8,128)} negate(f32[1,360,640]{2,1,0:T(8,128)} %shard_map.100) | non-fusion elementwise | flops 230400 | bytes 1843200 | tf_op jit(solution)/shard_map/neg | solution.py:376
